TPU v7x, 128 devices: a whole 4x4x4 slice. The times are simulated.
128 devices in a mesh: mem: 32 (over z, x, core), tile: 4 (over y).
Axes of the slice: x: 4, y: 4, z: 4, core: 2. Of those that a mesh axis runs over, the one named last changes fastest.
Arguments:
- background: float32 [2048, 8192], P('tile', 'mem'), may hold values from -21 to 21
- obs_value: float32 [2048, 128], P('tile', 'mem'), may hold values from -6 to 6
- obs_height: float32 [2048, 128], P('tile', 'mem'), may hold values from 0 to 63
- obs_weight: float32 [2048, 128], P('tile', 'mem'), may hold values from 0.25 to 2
- counts: int32 [2048], P('tile'), may hold values from 1 to 128
- owner: int32 [2048, 1], P('tile'), may hold values from 0 to 127; in each aligned block of 512 rows (0 to 511, 512 to 1023, ...) at most 8 rows name the same one
- loc_index: int32 [2048, 128], P('tile', 'mem'), may hold values from 0 to 15
- loc_table: float32 [16], replicated, may hold values from 0.05 to 1
Outputs:
- analysis: float32 [2048, 8192], P('tile', 'mem')
- owner_load: float32 [128], P(('mem', 'tile'))
Inputs may be any that keep to these rules, and one draw needn't show every extreme that they name: Among the columns of one tile at most 8 name the same owner, a bound that some tile reaches.
All inputs are finite; a program needn't handle non-finite values.
Results may differ from a plain program's by a relative error of at most 0.00023.
Values sent between devices are 32-bit elements; how exact they have to be, the bound alone decides.
A program may use at most 64 MiB of HBM per device.

v0:
```python
import functools

import jax
import jax.numpy as jnp
from jax import lax
from jax.experimental import pallas as pl
from jax.experimental.pallas import tpu as pltpu
from jax.sharding import PartitionSpec as P

LEV = 64
OBS = 128
LOC_N = 16
CAP = 8
N_MEM = 32
N_TILE = 4
COLS_T = 512
OWN = COLS_T // N_MEM
CHUNK = 8
CHUNKS = OWN // CHUNK
OBS_L = OBS // N_MEM
WIDTH = 256

F32 = jnp.float32
BF16 = jnp.bfloat16
MESH = pl.DeviceIdType.MESH


def iota(shape, axis):
    return lax.broadcasted_iota(jnp.int32, shape, axis)


def split(x):
    high = x.astype(BF16)
    return high, (x - high.astype(F32)).astype(BF16)


def right_side(x, keep0, keep1):
    high, low = split(x)
    top = jnp.concatenate([high * keep0, low * keep0], 1)
    bottom = jnp.concatenate([high * keep1, low * keep1], 1)
    return jnp.concatenate([top, bottom, top, bottom], 0)


def product(a, right):
    high, low = split(a)
    both = jnp.dot(jnp.concatenate([high, low], 1), right, preferred_element_type=F32)
    return both[:, :128] + both[:, 128:]


def analyse(blocks, values, heights, weights):
    n = len(blocks)
    lane = iota((64, 128), 1)
    row = iota((64, 128), 0)
    left = lane < 64
    left1 = left[:1]
    keep0 = jnp.where(left, 1.0, 0.0).astype(BF16)
    keep1 = jnp.where(left, 0.0, 1.0).astype(BF16)
    eye = jnp.where((lane & 63) == row, 1.0, 0.0)
    eye_left = jnp.where(lane == row, 1.0, 0.0)
    level = row.astype(F32)
    perturb, centre, square, diag, off, force = [], [], [], [], [], []
    for i in range(n):
        x = jnp.concatenate([blocks[i][:, :128], blocks[i][:, 128:]], 0)
        total = jnp.sum(x, 0, keepdims=True)
        mean = (total + pltpu.roll(total, 64, 1)) * (1.0 / 128.0)
        x = x - mean
        high, low = split(x)
        square.append(
            lax.dot_general(
                jnp.concatenate([high, high, low, low], 0),
                jnp.concatenate([high, low, high, low], 0),
                (((0,), (0,)), ((), ())),
                preferred_element_type=F32,
            )
        )
        hat = jnp.maximum(0.0, 1.0 - jnp.abs(level - heights[i]))
        hat_next = jnp.maximum(0.0, 1.0 - jnp.abs((level + 1.0) - heights[i]))
        weighted = weights[i] * hat
        diag.append(jnp.sum(weighted * hat, 1, keepdims=True))
        off.append(jnp.sum(weighted * hat_next, 1, keepdims=True))
        mean_col = jnp.sum(eye_left * mean, 1, keepdims=True)
        innovation = values[i] - jnp.sum(hat * mean_col, 0, keepdims=True)
        force.append(jnp.sum(weighted * innovation, 1, keepdims=True))
        perturb.append(x)
        centre.append(mean)
    base, force_row = [], []
    for i in range(0, n, 2):
        j = i + 1
        g = jnp.where(left, square[i][:64], square[j][64:]) + pltpu.roll(
            jnp.where(left, square[j][:64], square[i][64:]), 64, 1
        )
        d = jnp.where(left, diag[i], diag[j])
        e = jnp.where(left, off[i], off[j])
        w = jnp.where(left, force[i], force[j])
        base.append(d * g + pltpu.roll(e * g, 1, 0) + e * pltpu.roll(g, 63, 0))
        force_row.append(jnp.broadcast_to(jnp.sum(w * g, 0, keepdims=True), (16, 128)))
    y, z, t, inverse = [], [], [], []
    for b, w in zip(base, force_row):
        out = product(jnp.concatenate([b, w], 0), right_side(b, keep0, keep1))
        b2, wb = out[:64], out[64:]
        trace = jnp.sum(eye * (254.0 * b + b2), 0, keepdims=True)
        norm2 = 127.0 * 127.0 * 128.0 + jnp.where(
            left1,
            jnp.sum(jnp.where(left1, trace, 0.0), 1, keepdims=True),
            jnp.sum(jnp.where(left1, 0.0, trace), 1, keepdims=True),
        )
        a = lax.rsqrt(norm2)
        c = (127.0 * eye + b) * a
        c2 = (16129.0 * eye + 254.0 * b + b2) * (a * a)
        y.append(1.5 * c - 0.5 * c2)
        z.append(1.5 * eye - 0.5 * c)
        t.append(1.5 * w - (0.5 * a) * (127.0 * w + wb))
        inverse.append(a)
    pairs = range(len(y))
    for sweep in range(4):
        middle = [
            1.5 * eye - 0.5 * product(z[q], right_side(y[q], keep0, keep1)) for q in pairs
        ]
        for q in pairs:
            right = right_side(middle[q], keep0, keep1)
            if sweep < 3:
                out = product(jnp.concatenate([y[q], z[q], t[q]], 0), right)
                y[q], z[q], t[q] = out[:64], out[64:128], out[128:]
            else:
                out = product(jnp.concatenate([z[q], t[q]], 0), right)
                z[q], t[q] = out[:64], out[64:]
    results = []
    for q in pairs:
        swapped = pltpu.roll(z[q], 64, 1)
        scale = jnp.sqrt(127.0 * inverse[q])
        scale_swapped = pltpu.roll(scale, 64, 1)
        for j in (0, 1):
            i = 2 * q + j
            mine = left if j == 0 else ~left
            mine1 = mine[:1]
            right = right_side(jnp.where(mine, z[q], swapped), keep0, keep1)
            out = product(jnp.concatenate([perturb[i], t[q]], 0), right)
            shift = inverse[q] * out[64:65]
            shift = jnp.where(mine1, shift, pltpu.roll(shift, 64, 1))
            factor = jnp.where(mine1, scale, scale_swapped)
            full = (centre[i] + shift) + factor * out[:64]
            results.append(jnp.concatenate([full[:32], full[32:]], 1))
    return results


def swap_blocks(x):
    row = iota(x.shape, 0)
    block = iota(x.shape, 1) // 16
    for s in (1, 2, 4):
        row_bit = (row // s) % 2
        block_bit = (block // s) % 2
        up = pltpu.roll(pltpu.roll(x, 64 - s, 0), 16 * s, 1)
        down = pltpu.roll(pltpu.roll(x, s, 0), 128 - 16 * s, 1)
        x = jnp.where(row_bit == block_bit, x, jnp.where(row_bit < block_bit, up, down))
    return x


def offsets():
    every = [(z, x, c) for z in range(4) for x in range(4) for c in range(2) if z or x or c]
    return sorted(every, key=lambda o: (-(min(o[0], 4 - o[0]) + min(o[1], 4 - o[1])), o[2]))


def kernel(
    bg, value, height, obs_weight, index, counts, owner, table, out, load_out,
    value_v, height_v, weight_v, index_v, counts_v, owner_v, table_v,
    message, received, fields, load_send, load_recv, rows_in, rows_out,
    small_sem, in_send, in_recv, out_send, out_recv, obs_send, obs_recv, load_sems,
):
    me = lax.axis_index("mem")
    tile = lax.axis_index("tile")
    z, x, core = me // 8, (me // 2) % 4, me % 2
    partners = [
        ((z + dz) % 4) * 8 + ((x + dx) % 4) * 2 + (core + dc) % 2 for dz, dx, dc in offsets()
    ]
    tile_partners = [(tile + d) % N_TILE for d in range(1, N_TILE)]
    small = [
        pltpu.make_async_copy(a, b, small_sem.at[i])
        for i, (a, b) in enumerate(
            zip(
                (value, height, obs_weight, index, counts, owner, table),
                (value_v, height_v, weight_v, index_v, counts_v, owner_v, table_v),
            )
        )
    ]
    for copy in small:
        copy.start()
    barrier = pltpu.get_barrier_semaphore()
    for p in partners:
        pl.semaphore_signal(barrier, inc=1, device_id=(p, tile), device_id_type=MESH)
    for q in tile_partners:
        pl.semaphore_signal(barrier, inc=1, device_id=(me, q), device_id_type=MESH)
    for copy in small:
        copy.wait()

    localised = jnp.zeros((OBS_L, COLS_T), F32)
    entry = index_v[...]
    table_row = table_v[...]
    for k in range(LOC_N):
        localised = jnp.where(entry == k, table_row[:, k : k + 1], localised)
    live = (me * OBS_L + iota((OBS_L, COLS_T), 0)) < counts_v[...]
    weights = jnp.where(live, localised * weight_v[...], 0.0)
    first = jnp.concatenate([value_v[...], height_v[...]], 0)
    second = jnp.concatenate([weights, jnp.zeros((OBS_L, COLS_T), F32)], 0)
    stack = []
    for b in range(4):
        stack += [first[:, 128 * b : 128 * b + 128], second[:, 128 * b : 128 * b + 128]]
    stack = swap_blocks(jnp.concatenate(stack, 0))
    column_load = jnp.sum(weights, 0, keepdims=True)
    right_half = jnp.concatenate([stack[16 * b + 8 : 16 * b + 16] for b in range(4)], 0)
    lane = iota((N_MEM, 128), 1)
    first_owner = iota((N_MEM, COLS_T), 0) * N_TILE
    owners = owner_v[...]
    for q in range(N_TILE):
        part = jnp.sum(
            jnp.where(first_owner + q == owners, column_load, 0.0), 1, keepdims=True
        )
        right_half = jnp.where(lane == 64 + q, part, right_half)
    left_half = jnp.concatenate([stack[16 * b : 16 * b + 8] for b in range(4)], 0)
    message[...] = jnp.concatenate([left_half, right_half], 1).reshape(N_MEM, 1, WIDTH)

    pl.semaphore_wait(barrier, N_MEM - 1 + N_TILE - 1)

    def send_rows(c):
        def source(p):
            return bg.at[pl.ds(pl.multiple_of(p * OWN + c * CHUNK, CHUNK), CHUNK)]

        for p in partners:
            pltpu.make_async_remote_copy(
                src_ref=source(p),
                dst_ref=rows_in.at[c, me],
                send_sem=in_send.at[c],
                recv_sem=in_recv.at[c],
                device_id=(p, tile),
                device_id_type=MESH,
            ).start()
        pltpu.make_async_copy(source(me), rows_in.at[c, me], in_recv.at[c]).start()

    send_rows(0)
    for p in partners:
        pltpu.make_async_remote_copy(
            src_ref=message.at[p],
            dst_ref=received.at[me],
            send_sem=obs_send,
            recv_sem=obs_recv,
            device_id=(p, tile),
            device_id_type=MESH,
        ).start()
    pltpu.make_async_copy(message.at[me], received.at[me], obs_recv).start()
    for c in range(1, CHUNKS):
        send_rows(c)

    pltpu.make_async_copy(received, received, obs_recv).wait()
    arrived = received[...].reshape(N_MEM, WIDTH)
    arrived = jnp.concatenate([arrived, jnp.zeros((128 - N_MEM, WIDTH), F32)], 0).T
    for f in range(3):
        fields[f] = jnp.concatenate(
            [arrived[(4 * f + o) * OWN : (4 * f + o + 1) * OWN, :N_MEM] for o in range(OBS_L)], 1
        )
    loads = jnp.sum(arrived[192 : 192 + N_TILE], 1, keepdims=True)
    load_send[...] = jnp.broadcast_to(loads, (N_TILE, 128)).reshape(N_TILE, 1, 128)
    for q in tile_partners:
        pltpu.make_async_remote_copy(
            src_ref=load_send.at[q],
            dst_ref=load_recv.at[tile],
            send_sem=load_sems.at[0],
            recv_sem=load_sems.at[1],
            device_id=(me, q),
            device_id_type=MESH,
        ).start()
    pltpu.make_async_copy(load_send.at[tile], load_recv.at[tile], load_sems.at[1]).start()

    def step(c, carry):
        pltpu.make_async_copy(rows_in.at[c], rows_in.at[c], in_recv.at[c]).wait()
        base = pl.multiple_of(c * CHUNK, CHUNK)
        obs = [fields[f, pl.ds(base, CHUNK)] for f in range(3)]
        results = analyse(
            [rows_in[c, :, i, :] for i in range(CHUNK)],
            *[[a[i : i + 1] for i in range(CHUNK)] for a in obs],
        )
        for i in range(CHUNK):
            rows_out[c, :, i, :] = results[i]
        target = out.at[pl.ds(pl.multiple_of(me * OWN + c * CHUNK, CHUNK), CHUNK)]
        for p in partners:
            pltpu.make_async_remote_copy(
                src_ref=rows_out.at[c, p],
                dst_ref=target,
                send_sem=out_send.at[c],
                recv_sem=out_recv.at[c],
                device_id=(p, tile),
                device_id_type=MESH,
            ).start()
        pltpu.make_async_copy(rows_out.at[c, me], target, out_recv.at[c]).start()
        return carry

    lax.fori_loop(0, CHUNKS, step, 0)

    pltpu.make_async_copy(load_recv, load_recv, load_sems.at[1]).wait()
    load_out[...] = jnp.sum(load_recv[...], 0)[:, :1] * (1.0 / (OBS * CAP))
    sent = load_send.at[pl.ds(0, N_TILE - 1)]
    pltpu.make_async_copy(sent, sent, load_sems.at[0]).wait()
    sent = message.at[pl.ds(0, N_MEM - 1)]
    pltpu.make_async_copy(sent, sent, obs_send).wait()
    for c in range(CHUNKS):
        sent = rows_in.at[c, pl.ds(0, N_MEM - 1)]
        pltpu.make_async_copy(sent, sent, in_send.at[c]).wait()
        pltpu.make_async_copy(sent, sent, out_send.at[c]).wait()
        pltpu.make_async_copy(rows_out.at[c], rows_out.at[c], out_recv.at[c]).wait()


def per_device(background, obs_value, obs_height, obs_weight, counts, owner, loc_index, loc_table):
    hbm = pl.BlockSpec(memory_space=pl.ANY)
    dma = pltpu.SemaphoreType.DMA
    analysis, load = pl.pallas_call(
        kernel,
        out_shape=(
            jax.ShapeDtypeStruct((COLS_T, WIDTH), F32),
            jax.ShapeDtypeStruct((1, 1), F32),
        ),
        in_specs=[hbm] * 8,
        out_specs=(hbm, pl.BlockSpec(memory_space=pltpu.VMEM)),
        scratch_shapes=[
            pltpu.VMEM((OBS_L, COLS_T), F32),
            pltpu.VMEM((OBS_L, COLS_T), F32),
            pltpu.VMEM((OBS_L, COLS_T), F32),
            pltpu.VMEM((OBS_L, COLS_T), jnp.int32),
            pltpu.VMEM((1, COLS_T), jnp.int32),
            pltpu.VMEM((1, COLS_T), jnp.int32),
            pltpu.VMEM((1, LOC_N), F32),
            pltpu.VMEM((N_MEM, 1, WIDTH), F32),
            pltpu.VMEM((N_MEM, 1, WIDTH), F32),
            pltpu.VMEM((3, OWN, OBS), F32),
            pltpu.VMEM((N_TILE, 1, 128), F32),
            pltpu.VMEM((N_TILE, 1, 128), F32),
            pltpu.VMEM((CHUNKS, N_MEM, CHUNK, WIDTH), F32),
            pltpu.VMEM((CHUNKS, N_MEM, CHUNK, WIDTH), F32),
            dma((7,)),
            dma((CHUNKS,)),
            dma((CHUNKS,)),
            dma((CHUNKS,)),
            dma((CHUNKS,)),
            dma,
            dma,
            dma((2,)),
        ],
        compiler_params=pltpu.CompilerParams(
            collective_id=0, has_side_effects=True, vmem_limit_bytes=60 << 20
        ),
    )(
        background,
        obs_value.T,
        obs_height.T,
        obs_weight.T,
        loc_index.T,
        counts.reshape(1, COLS_T),
        owner.reshape(1, COLS_T),
        loc_table.reshape(1, LOC_N),
    )
    return analysis, load.reshape(1)


def solution(mesh):
    placed = (
        P("tile", "mem"),
        P("tile", "mem"),
        P("tile", "mem"),
        P("tile", "mem"),
        P("tile"),
        P("tile", None),
        P("tile", "mem"),
        P(),
    )
    return jax.shard_map(
        per_device,
        mesh=mesh,
        in_specs=placed,
        out_specs=(P("tile", "mem"), P(("mem", "tile"))),
        check_vma=False,
    )
```

profile of v0, /device:TPU:1, one launch (start us, length us, event | category | flops | bytes accessed | tf_op | source)
XLA Modules:
  0.0 32.4 jit_solution(13999155460644446432)
XLA Ops:
  0.6 28.2 %shard_map.95 = (f32[512,256]{1,0:T(8,128)}, f32[1,1]{1,0:T(1,128)}) custom-call(f32[512,256]{1,0:T(8,128)} %bg.1, f32[4,512]{1,0:T(4,128)} %bitcast.8, f32[4,512]{1,0:T(4,128)} %bitcast.9, f32[4,512]{1,0:T(4,128)} %bitcast.10, s32[4,512]{1,0:T(4,128)} %bitcast.11, s32[1,512]{1,0:T(1,128)} %bitcast.12, s32[1,512]{1,0:T(1,128)} %bitcast.13, f32[1,16]{1,0:T(1,128)} %bitcast.14), custom_call_target="tpu_custom_call" | custom-call | tf_op jit(solution)/shard_map/pallas_call | solution.py:313
  28.8 1.9 %copy.12 = f32[512,256]{1,0:T(8,128)} copy(f32[512,256]{1,0:T(8,128)} %get-tuple-element.8) | data formatting | bytes 1048576
where the time goes:
time: 32.6 us; the launch traced here: 32.4 us
  Pallas kernels  28.2 us (87%)
  between operations  2.34 us (7%)
  local copies, waits for them, and re-layouts  1.87 us (6%)
    pallas_call x1, Pallas kernels, per_device(): pl.pallas_call(kernel, out_shape=(jax.ShapeDtypeStruct((COLS_T, WIDTH), F...  28.2 us
    unnamed x1, local copies, waits for them, and re-layouts  1.87 us

commit v1 on v0

--- a/solution.py
+++ b/solution.py
@@ -47,57 +47,80 @@
     return both[:, :128] + both[:, 128:]
 
 
-def analyse(blocks, values, heights, weights):
-    n = len(blocks)
+def lane_masks():
     lane = iota((64, 128), 1)
-    row = iota((64, 128), 0)
     left = lane < 64
-    left1 = left[:1]
     keep0 = jnp.where(left, 1.0, 0.0).astype(BF16)
     keep1 = jnp.where(left, 0.0, 1.0).astype(BF16)
+    return lane, iota((64, 128), 0), left, keep0, keep1
+
+
+def observe(fields, shared):
+    left = lane_masks()[2]
+    level = iota((64, 128), 0).astype(F32)
+
+    def pair(q, carry):
+        both = []
+        for j in (0, 1):
+            value, height, weight = [fields[f, pl.ds(2 * q + j, 1), :] for f in range(3)]
+            hat = jnp.maximum(0.0, 1.0 - jnp.abs(level - height))
+            hat_next = jnp.maximum(0.0, 1.0 - jnp.abs((level + 1.0) - height))
+            weighted = weight * hat
+            terms = (weighted * hat, weighted * hat_next, weighted * value)
+            both.append([jnp.sum(x, 1, keepdims=True) for x in terms])
+        for k in range(3):
+            shared[q, k] = jnp.where(left, both[0][k], both[1][k])
+        return carry
+
+    lax.fori_loop(0, OWN // 2, pair, 0)
+
+
+def analyse(blocks, shared):
+    lane, row, left, keep0, keep1 = lane_masks()
+    left1 = left[:1]
     eye = jnp.where((lane & 63) == row, 1.0, 0.0)
     eye_left = jnp.where(lane == row, 1.0, 0.0)
-    level = row.astype(F32)
-    perturb, centre, square, diag, off, force = [], [], [], [], [], []
-    for i in range(n):
-        x = jnp.concatenate([blocks[i][:, :128], blocks[i][:, 128:]], 0)
+    pairs = range(len(shared))
+
+    def own(x, j):
+        return jnp.where(left[: x.shape[0]] == (j == 0), x, pltpu.roll(x, 64, 1))
+
+    halves, centre, square, mean_col = [], [], [], []
+    for block in blocks:
+        x = jnp.concatenate([block[:, :128], block[:, 128:]], 0)
         total = jnp.sum(x, 0, keepdims=True)
         mean = (total + pltpu.roll(total, 64, 1)) * (1.0 / 128.0)
-        x = x - mean
-        high, low = split(x)
-        square.append(
-            lax.dot_general(
-                jnp.concatenate([high, high, low, low], 0),
-                jnp.concatenate([high, low, high, low], 0),
-                (((0,), (0,)), ((), ())),
-                preferred_element_type=F32,
-            )
-        )
-        hat = jnp.maximum(0.0, 1.0 - jnp.abs(level - heights[i]))
-        hat_next = jnp.maximum(0.0, 1.0 - jnp.abs((level + 1.0) - heights[i]))
-        weighted = weights[i] * hat
-        diag.append(jnp.sum(weighted * hat, 1, keepdims=True))
-        off.append(jnp.sum(weighted * hat_next, 1, keepdims=True))
-        mean_col = jnp.sum(eye_left * mean, 1, keepdims=True)
-        innovation = values[i] - jnp.sum(hat * mean_col, 0, keepdims=True)
-        force.append(jnp.sum(weighted * innovation, 1, keepdims=True))
-        perturb.append(x)
+        high, low = split(x - mean)
+        both = lax.dot_general(
+            jnp.concatenate([high, low], 0),
+            jnp.concatenate([jnp.concatenate([high, low], 1)] * 2, 0),
+            (((0,), (0,)), ((), ())),
+            preferred_element_type=F32,
+        )
+        square.append(both[:, :128] + both[:, 128:])
+        mean_col.append(jnp.sum(eye_left * mean, 1, keepdims=True))
+        halves.append(jnp.concatenate([high, low], 1))
         centre.append(mean)
-    base, force_row = [], []
-    for i in range(0, n, 2):
-        j = i + 1
+    base, force = [], []
+    for q in pairs:
+        i, j = 2 * q, 2 * q + 1
         g = jnp.where(left, square[i][:64], square[j][64:]) + pltpu.roll(
             jnp.where(left, square[j][:64], square[i][64:]), 64, 1
         )
-        d = jnp.where(left, diag[i], diag[j])
-        e = jnp.where(left, off[i], off[j])
-        w = jnp.where(left, force[i], force[j])
-        base.append(d * g + pltpu.roll(e * g, 1, 0) + e * pltpu.roll(g, 63, 0))
-        force_row.append(jnp.broadcast_to(jnp.sum(w * g, 0, keepdims=True), (16, 128)))
-    y, z, t, inverse = [], [], [], []
-    for b, w in zip(base, force_row):
-        out = product(jnp.concatenate([b, w], 0), right_side(b, keep0, keep1))
-        b2, wb = out[:64], out[64:]
+        d, e, w = shared[q]
+
+        def tridiagonal(m):
+            return d * m + pltpu.roll(e * m, 1, 0) + e * pltpu.roll(m, 63, 0)
+
+        w = w - tridiagonal(jnp.where(left, mean_col[i], mean_col[j]))
+        base.append(tridiagonal(g))
+        force.append(jnp.broadcast_to(jnp.sum(w * g, 0, keepdims=True), (16, 128)))
+    right = [right_side(b, keep0, keep1) for b in base]
+    out = [product(jnp.concatenate([base[q], force[q]], 0), right[q]) for q in pairs]
+    cube = [product(out[q][:64], right[q]) for q in pairs]
+    p, z, t, inverse = [], [], [], []
+    for q in pairs:
+        b, b2 = base[q], out[q][:64]
         trace = jnp.sum(eye * (254.0 * b + b2), 0, keepdims=True)
         norm2 = 127.0 * 127.0 * 128.0 + jnp.where(
             left1,
@@ -105,40 +128,41 @@
             jnp.sum(jnp.where(left1, 0.0, trace), 1, keepdims=True),
         )
         a = lax.rsqrt(norm2)
-        c = (127.0 * eye + b) * a
-        c2 = (16129.0 * eye + 254.0 * b + b2) * (a * a)
-        y.append(1.5 * c - 0.5 * c2)
-        z.append(1.5 * eye - 0.5 * c)
-        t.append(1.5 * w - (0.5 * a) * (127.0 * w + wb))
+        u = 127.0 * a
+        p.append(
+            (u * (2.25 + u * (-1.5 + 0.25 * u))) * eye
+            + (a * (2.25 + u * (-3.0 + 0.75 * u))) * b
+            + (a * a * (-1.5 + 0.75 * u)) * b2
+            + (a * a * a * 0.25) * cube[q]
+        )
+        z.append((1.5 - 0.5 * u) * eye - (0.5 * a) * b)
+        t.append((1.5 - 0.5 * u) * force[q] - (0.5 * a) * out[q][64:])
         inverse.append(a)
-    pairs = range(len(y))
-    for sweep in range(4):
-        middle = [
-            1.5 * eye - 0.5 * product(z[q], right_side(y[q], keep0, keep1)) for q in pairs
-        ]
+    for sweep in range(3):
+        right = [right_side(p[q], keep0, keep1) for q in pairs]
+        out = [product(jnp.concatenate([p[q], z[q], t[q]], 0), right[q]) for q in pairs]
+        cube = [product(out[q][:64], right[q]) for q in pairs]
         for q in pairs:
-            right = right_side(middle[q], keep0, keep1)
-            if sweep < 3:
-                out = product(jnp.concatenate([y[q], z[q], t[q]], 0), right)
-                y[q], z[q], t[q] = out[:64], out[64:128], out[128:]
-            else:
-                out = product(jnp.concatenate([z[q], t[q]], 0), right)
-                z[q], t[q] = out[:64], out[64:]
+            z[q] = 1.5 * z[q] - 0.5 * out[q][64:128]
+            t[q] = 1.5 * t[q] - 0.5 * out[q][128:]
+            p[q] = 2.25 * p[q] - 1.5 * out[q][:64] + 0.25 * cube[q]
     results = []
     for q in pairs:
-        swapped = pltpu.roll(z[q], 64, 1)
+        out = product(jnp.concatenate([z[q], t[q]], 0), right_side(p[q], keep0, keep1))
+        z[q] = 1.5 * z[q] - 0.5 * out[:64]
+        t[q] = 1.5 * t[q] - 0.5 * out[64:]
+    for q in pairs:
         scale = jnp.sqrt(127.0 * inverse[q])
-        scale_swapped = pltpu.roll(scale, 64, 1)
+        t_halves = jnp.concatenate(split(t[q]), 1)
         for j in (0, 1):
             i = 2 * q + j
-            mine = left if j == 0 else ~left
-            mine1 = mine[:1]
-            right = right_side(jnp.where(mine, z[q], swapped), keep0, keep1)
-            out = product(jnp.concatenate([perturb[i], t[q]], 0), right)
-            shift = inverse[q] * out[64:65]
-            shift = jnp.where(mine1, shift, pltpu.roll(shift, 64, 1))
-            factor = jnp.where(mine1, scale, scale_swapped)
-            full = (centre[i] + shift) + factor * out[:64]
+            both = jnp.dot(
+                jnp.concatenate([halves[i], t_halves], 0),
+                right_side(own(z[q], j), keep0, keep1),
+                preferred_element_type=F32,
+            )
+            both = both[:, :128] + both[:, 128:]
+            full = (centre[i] + own(inverse[q] * both[64:65], j)) + own(scale, j) * both[:64]
             results.append(jnp.concatenate([full[:32], full[32:]], 1))
     return results
 
@@ -161,18 +185,19 @@
 
 
 def kernel(
-    bg, value, height, obs_weight, index, counts, owner, table, out, load_out,
+    bg, value, height, obs_weight, index, counts, owner, table, out, load_recv,
     value_v, height_v, weight_v, index_v, counts_v, owner_v, table_v,
-    message, received, fields, load_send, load_recv, rows_in, rows_out,
+    message, received, fields, shared, load_send, rows_in, rows_out,
     small_sem, in_send, in_recv, out_send, out_recv, obs_send, obs_recv, load_sems,
 ):
     me = lax.axis_index("mem")
     tile = lax.axis_index("tile")
     z, x, core = me // 8, (me // 2) % 4, me % 2
-    partners = [
-        ((z + dz) % 4) * 8 + ((x + dx) % 4) * 2 + (core + dc) % 2 for dz, dx, dc in offsets()
-    ]
-    tile_partners = [(tile + d) % N_TILE for d in range(1, N_TILE)]
+    zs = [lax.rem(z + d, 4) * 8 for d in range(4)]
+    xs = [lax.rem(x + d, 4) * 2 for d in range(4)]
+    cores = [core, 1 - core]
+    partners = [zs[dz] + (xs[dx] + cores[dc]) for dz, dx, dc in offsets()]
+    tile_partners = [lax.rem(tile + d, N_TILE) for d in range(1, N_TILE)]
     small = [
         pltpu.make_async_copy(a, b, small_sem.at[i])
         for i, (a, b) in enumerate(
@@ -235,7 +260,6 @@
             ).start()
         pltpu.make_async_copy(source(me), rows_in.at[c, me], in_recv.at[c]).start()
 
-    send_rows(0)
     for p in partners:
         pltpu.make_async_remote_copy(
             src_ref=message.at[p],
@@ -246,7 +270,7 @@
             device_id_type=MESH,
         ).start()
     pltpu.make_async_copy(message.at[me], received.at[me], obs_recv).start()
-    for c in range(1, CHUNKS):
+    for c in range(CHUNKS):
         send_rows(c)
 
     pltpu.make_async_copy(received, received, obs_recv).wait()
@@ -269,13 +293,16 @@
         ).start()
     pltpu.make_async_copy(load_send.at[tile], load_recv.at[tile], load_sems.at[1]).start()
 
+    observe(fields, shared)
+
     def step(c, carry):
         pltpu.make_async_copy(rows_in.at[c], rows_in.at[c], in_recv.at[c]).wait()
-        base = pl.multiple_of(c * CHUNK, CHUNK)
-        obs = [fields[f, pl.ds(base, CHUNK)] for f in range(3)]
         results = analyse(
             [rows_in[c, :, i, :] for i in range(CHUNK)],
-            *[[a[i : i + 1] for i in range(CHUNK)] for a in obs],
+            [
+                [shared[c * (CHUNK // 2) + q, k] for k in range(3)]
+                for q in range(CHUNK // 2)
+            ],
         )
         for i in range(CHUNK):
             rows_out[c, :, i, :] = results[i]
@@ -295,7 +322,6 @@
     lax.fori_loop(0, CHUNKS, step, 0)
 
     pltpu.make_async_copy(load_recv, load_recv, load_sems.at[1]).wait()
-    load_out[...] = jnp.sum(load_recv[...], 0)[:, :1] * (1.0 / (OBS * CAP))
     sent = load_send.at[pl.ds(0, N_TILE - 1)]
     pltpu.make_async_copy(sent, sent, load_sems.at[0]).wait()
     sent = message.at[pl.ds(0, N_MEM - 1)]
@@ -307,17 +333,31 @@
         pltpu.make_async_copy(rows_out.at[c], rows_out.at[c], out_recv.at[c]).wait()
 
 
+def finish(rows, parts, out, load_out, load_v, sems):
+    rows_copy = pltpu.make_async_copy(rows, out, sems.at[0])
+    rows_copy.start()
+    load_v[...] = jnp.sum(parts[...], 0) * (1.0 / (OBS * CAP))
+    load_copy = pltpu.make_async_copy(load_v, load_out, sems.at[1])
+    load_copy.start()
+    rows_copy.wait()
+    load_copy.wait()
+
+
 def per_device(background, obs_value, obs_height, obs_weight, counts, owner, loc_index, loc_table):
     hbm = pl.BlockSpec(memory_space=pl.ANY)
+
+    def keep(x):
+        return pltpu.with_memory_space_constraint(x, pltpu.HBM)
+
     dma = pltpu.SemaphoreType.DMA
     analysis, load = pl.pallas_call(
         kernel,
         out_shape=(
             jax.ShapeDtypeStruct((COLS_T, WIDTH), F32),
-            jax.ShapeDtypeStruct((1, 1), F32),
+            jax.ShapeDtypeStruct((N_TILE, 1, 128), F32),
         ),
         in_specs=[hbm] * 8,
-        out_specs=(hbm, pl.BlockSpec(memory_space=pltpu.VMEM)),
+        out_specs=(hbm, hbm),
         scratch_shapes=[
             pltpu.VMEM((OBS_L, COLS_T), F32),
             pltpu.VMEM((OBS_L, COLS_T), F32),
@@ -329,7 +369,7 @@
             pltpu.VMEM((N_MEM, 1, WIDTH), F32),
             pltpu.VMEM((N_MEM, 1, WIDTH), F32),
             pltpu.VMEM((3, OWN, OBS), F32),
-            pltpu.VMEM((N_TILE, 1, 128), F32),
+            pltpu.VMEM((OWN // 2, 3, 64, 128), F32),
             pltpu.VMEM((N_TILE, 1, 128), F32),
             pltpu.VMEM((CHUNKS, N_MEM, CHUNK, WIDTH), F32),
             pltpu.VMEM((CHUNKS, N_MEM, CHUNK, WIDTH), F32),
@@ -343,19 +383,30 @@
             dma((2,)),
         ],
         compiler_params=pltpu.CompilerParams(
-            collective_id=0, has_side_effects=True, vmem_limit_bytes=60 << 20
+            collective_id=0, has_side_effects=True, vmem_limit_bytes=16 << 20
         ),
     )(
-        background,
-        obs_value.T,
-        obs_height.T,
-        obs_weight.T,
-        loc_index.T,
-        counts.reshape(1, COLS_T),
-        owner.reshape(1, COLS_T),
-        loc_table.reshape(1, LOC_N),
+        keep(background),
+        keep(obs_value.T),
+        keep(obs_height.T),
+        keep(obs_weight.T),
+        keep(loc_index.T),
+        keep(counts.reshape(1, COLS_T)),
+        keep(owner.reshape(1, COLS_T)),
+        keep(loc_table.reshape(1, LOC_N)),
     )
-    return analysis, load.reshape(1)
+    analysis, load = pl.pallas_call(
+        finish,
+        out_shape=(
+            jax.ShapeDtypeStruct((COLS_T, WIDTH), F32),
+            jax.ShapeDtypeStruct((1, 128), F32),
+        ),
+        in_specs=[hbm, pl.BlockSpec(memory_space=pltpu.VMEM)],
+        out_specs=(hbm, hbm),
+        scratch_shapes=[pltpu.VMEM((1, 128), F32), dma((2,))],
+        compiler_params=pltpu.CompilerParams(vmem_limit_bytes=16 << 20),
+    )(analysis, load)
+    return analysis, load[0, :1]
 
 
 def solution(mesh):

time: 32.6 us -> 27.3 us (0.84)
  local copies, waits for them, and re-layouts: 1.87 us -> 0 us
  between operations: 2.34 us -> 0.64 us
  Pallas kernels: 28.2 us -> 26.5 us
    pallas_call x1, Pallas kernels: 28.2 us -> 25.7 us  [per_device(): pl.pallas_call(kernel, out_shape=(jax.ShapeDtypeStruct((COLS_T, WIDTH), F...]
    unnamed x1 -> x0, local copies, waits for them, and re-layouts: 1.87 us -> none
    pallas_call x0 -> x1, Pallas kernels: none -> 0.81 us  [per_device(): pl.pallas_call(finish, out_shape=(jax.ShapeDtypeStruct((COLS_T, WIDTH), F...]
where the time goes in v1:
time: 27.3 us; the launch traced here: 27.1 us
  Pallas kernels  26.5 us (97%)
  between operations  0.64 us (2%)
    pallas_call x1, Pallas kernels, per_device(): pl.pallas_call(kernel, out_shape=(jax.ShapeDtypeStruct((COLS_T, WIDTH), F...  25.7 us
    pallas_call x1, Pallas kernels, per_device(): pl.pallas_call(finish, out_shape=(jax.ShapeDtypeStruct((COLS_T, WIDTH), F...  0.81 us

profile of v1, /device:TPU:1, one launch (start us, length us, event | category | flops | bytes accessed | tf_op | source)
XLA Modules:
  0.0 27.1 jit_solution(13153352235024577307)
XLA Ops:
  0.6 25.7 %shard_map.95 = (f32[512,256]{1,0:T(8,128)S(1)}, f32[4,1,128]{2,1,0:T(1,128)S(1)}) custom-call(f32[512,256]{1,0:T(8,128)} %bg.1, f32[4,512]{1,0:T(4,128)} %bitcast.9, f32[4,512]{1,0:T(4,128)} %bitcast.10, f32[4,512]{1,0:T(4,128)} %bitcast.11, s32[4,512]{1,0:T(4,128)} %bitcast.12, s32[1,512]{1,0:T(1,128)} %bitcast.13, s32[1,512]{1,0:T(1,128)} %bitcast.14, ...), custom_call_target="tpu_custom_call" | custom-call | tf_op jit(solution)/shard_map/pallas_call | solution.py:353
  26.3 0.8 %shard_map.96 = (f32[512,256]{1,0:T(8,128)}, f32[1,128]{1,0:T(1,128)}) custom-call(f32[512,256]{1,0:T(8,128)S(1)} %get-tuple-element.6.rows, f32[4,1,128]{2,1,0:T(1,128)S(1)} %get-tuple-element.7.parts), custom_call_target="tpu_custom_call" | custom-call | tf_op jit(solution)/shard_map/pallas_call | solution.py:398

commit v2 on v1

--- a/solution.py
+++ b/solution.py
@@ -19,6 +19,11 @@
 CHUNKS = OWN // CHUNK
 OBS_L = OBS // N_MEM
 WIDTH = 256
+BY_START = [
+    2 * chip + core
+    for chip in sorted(range(N_MEM // 2), key=lambda k: 1.1 * (k // 4) + 0.45 * (k % 4))
+    for core in (1, 0)
+]
 
 F32 = jnp.float32
 BF16 = jnp.bfloat16
@@ -79,17 +84,16 @@
     lane, row, left, keep0, keep1 = lane_masks()
     left1 = left[:1]
     eye = jnp.where((lane & 63) == row, 1.0, 0.0)
-    eye_left = jnp.where(lane == row, 1.0, 0.0)
     pairs = range(len(shared))
 
-    def own(x, j):
-        return jnp.where(left[: x.shape[0]] == (j == 0), x, pltpu.roll(x, 64, 1))
+    def exchange(x, y):
+        return jnp.where(left, x, pltpu.roll(y, 64, 1)), jnp.where(left, pltpu.roll(x, 64, 1), y)
 
     halves, centre, square, mean_col = [], [], [], []
-    for block in blocks:
-        x = jnp.concatenate([block[:, :128], block[:, 128:]], 0)
-        total = jnp.sum(x, 0, keepdims=True)
-        mean = (total + pltpu.roll(total, 64, 1)) * (1.0 / 128.0)
+    for q in pairs:
+        x, y = [jnp.concatenate([b[:, :128], b[:, 128:]], 0) for b in blocks[2 * q : 2 * q + 2]]
+        x = jnp.concatenate(exchange(x, y), 0)
+        mean = jnp.sum(x, 0, keepdims=True) * (1.0 / 128.0)
         high, low = split(x - mean)
         both = lax.dot_general(
             jnp.concatenate([high, low], 0),
@@ -98,21 +102,25 @@
             preferred_element_type=F32,
         )
         square.append(both[:, :128] + both[:, 128:])
-        mean_col.append(jnp.sum(eye_left * mean, 1, keepdims=True))
+        diagonal = eye * mean
+        mean_col.append(
+            jnp.where(
+                left,
+                jnp.sum(jnp.where(left, diagonal, 0.0), 1, keepdims=True),
+                jnp.sum(jnp.where(left, 0.0, diagonal), 1, keepdims=True),
+            )
+        )
         halves.append(jnp.concatenate([high, low], 1))
         centre.append(mean)
     base, force = [], []
     for q in pairs:
-        i, j = 2 * q, 2 * q + 1
-        g = jnp.where(left, square[i][:64], square[j][64:]) + pltpu.roll(
-            jnp.where(left, square[j][:64], square[i][64:]), 64, 1
-        )
+        g = jnp.where(left, square[q][:64], square[q][64:])
         d, e, w = shared[q]
 
         def tridiagonal(m):
             return d * m + pltpu.roll(e * m, 1, 0) + e * pltpu.roll(m, 63, 0)
 
-        w = w - tridiagonal(jnp.where(left, mean_col[i], mean_col[j]))
+        w = w - tridiagonal(mean_col[q])
         base.append(tridiagonal(g))
         force.append(jnp.broadcast_to(jnp.sum(w * g, 0, keepdims=True), (16, 128)))
     right = [right_side(b, keep0, keep1) for b in base]
@@ -152,18 +160,16 @@
         z[q] = 1.5 * z[q] - 0.5 * out[:64]
         t[q] = 1.5 * t[q] - 0.5 * out[64:]
     for q in pairs:
-        scale = jnp.sqrt(127.0 * inverse[q])
         t_halves = jnp.concatenate(split(t[q]), 1)
-        for j in (0, 1):
-            i = 2 * q + j
-            both = jnp.dot(
-                jnp.concatenate([halves[i], t_halves], 0),
-                right_side(own(z[q], j), keep0, keep1),
-                preferred_element_type=F32,
-            )
-            both = both[:, :128] + both[:, 128:]
-            full = (centre[i] + own(inverse[q] * both[64:65], j)) + own(scale, j) * both[:64]
-            results.append(jnp.concatenate([full[:32], full[32:]], 1))
+        both = jnp.dot(
+            jnp.concatenate([halves[q], t_halves], 0),
+            right_side(z[q], keep0, keep1),
+            preferred_element_type=F32,
+        )
+        both = both[:, :128] + both[:, 128:]
+        full = (centre[q] + inverse[q] * both[128:129]) + jnp.sqrt(127.0 * inverse[q]) * both[:128]
+        for x in exchange(full[:64], full[64:]):
+            results.append(jnp.concatenate([x[:32], x[32:]], 1))
     return results
 
 
@@ -196,7 +202,10 @@
     zs = [lax.rem(z + d, 4) * 8 for d in range(4)]
     xs = [lax.rem(x + d, 4) * 2 for d in range(4)]
     cores = [core, 1 - core]
-    partners = [zs[dz] + (xs[dx] + cores[dc]) for dz, dx, dc in offsets()]
+    partners = []
+    for dz, dx, dc in offsets():
+        chips = jnp.where(core == 0, zs[dz] + xs[dx], zs[-dx % 4] + xs[-dz % 4])
+        partners.append(chips + cores[dc])
     tile_partners = [lax.rem(tile + d, N_TILE) for d in range(1, N_TILE)]
     small = [
         pltpu.make_async_copy(a, b, small_sem.at[i])
@@ -307,7 +316,8 @@
         for i in range(CHUNK):
             rows_out[c, :, i, :] = results[i]
         target = out.at[pl.ds(pl.multiple_of(me * OWN + c * CHUNK, CHUNK), CHUNK)]
-        for p in partners:
+
+        def send_out(p):
             pltpu.make_async_remote_copy(
                 src_ref=rows_out.at[c, p],
                 dst_ref=target,
@@ -316,6 +326,9 @@
                 device_id=(p, tile),
                 device_id_type=MESH,
             ).start()
+
+        for p in BY_START:
+            pl.when(p != me)(functools.partial(send_out, p))
         pltpu.make_async_copy(rows_out.at[c, me], target, out_recv.at[c]).start()
         return carry
 

time: 27.3 us -> 26.7 us (0.978)
  Pallas kernels: 26.5 us -> 25.9 us
    pallas_call x1, Pallas kernels: 25.7 us -> 25.1 us  [per_device(): pl.pallas_call(kernel, out_shape=(jax.ShapeDtypeStruct((COLS_T, WIDTH), F...]
where the time goes in v2:
time: 26.7 us; the launch traced here: 26.6 us
  Pallas kernels  25.9 us (97%)
  between operations  0.64 us (2%)
    pallas_call x1, Pallas kernels, per_device(): pl.pallas_call(kernel, out_shape=(jax.ShapeDtypeStruct((COLS_T, WIDTH), F...  25.1 us
    pallas_call x1, Pallas kernels, per_device(): pl.pallas_call(finish, out_shape=(jax.ShapeDtypeStruct((COLS_T, WIDTH), F...  0.81 us

profile of v2, /device:TPU:1, one launch (start us, length us, event | category | flops | bytes accessed | tf_op | source)
XLA Modules:
  0.0 26.6 jit_solution(15149431875951618038)
XLA Ops:
  0.6 25.1 %shard_map.95 = (f32[512,256]{1,0:T(8,128)S(1)}, f32[4,1,128]{2,1,0:T(1,128)S(1)}) custom-call(f32[512,256]{1,0:T(8,128)} %bg.1, f32[4,512]{1,0:T(4,128)} %bitcast.9, f32[4,512]{1,0:T(4,128)} %bitcast.10, f32[4,512]{1,0:T(4,128)} %bitcast.11, s32[4,512]{1,0:T(4,128)} %bitcast.12, s32[1,512]{1,0:T(1,128)} %bitcast.13, s32[1,512]{1,0:T(1,128)} %bitcast.14, ...), custom_call_target="tpu_custom_call" | custom-call | tf_op jit(solution)/shard_map/pallas_call | solution.py:366
  25.7 0.8 %shard_map.96 = (f32[512,256]{1,0:T(8,128)}, f32[1,128]{1,0:T(1,128)}) custom-call(f32[512,256]{1,0:T(8,128)S(1)} %get-tuple-element.6.rows, f32[4,1,128]{2,1,0:T(1,128)S(1)} %get-tuple-element.7.parts), custom_call_target="tpu_custom_call" | custom-call | tf_op jit(solution)/shard_map/pallas_call | solution.py:411

commit v3 on v2

--- a/solution.py
+++ b/solution.py
@@ -194,7 +194,7 @@
     bg, value, height, obs_weight, index, counts, owner, table, out, load_recv,
     value_v, height_v, weight_v, index_v, counts_v, owner_v, table_v,
     message, received, fields, shared, load_send, rows_in, rows_out,
-    small_sem, in_send, in_recv, out_send, out_recv, obs_send, obs_recv, load_sems,
+    tile_ready, small_sem, in_send, in_recv, out_send, out_recv, obs_send, obs_recv, load_sems,
 ):
     me = lax.axis_index("mem")
     tile = lax.axis_index("tile")
@@ -221,8 +221,14 @@
     barrier = pltpu.get_barrier_semaphore()
     for p in partners:
         pl.semaphore_signal(barrier, inc=1, device_id=(p, tile), device_id_type=MESH)
+
+    def greet(there, semaphore, q):
+        @pl.when(there)
+        def _():
+            pl.semaphore_signal(semaphore, inc=1, device_id=(me, q), device_id_type=MESH)
+
     for q in tile_partners:
-        pl.semaphore_signal(barrier, inc=1, device_id=(me, q), device_id_type=MESH)
+        greet(q > tile, barrier, q)
     for copy in small:
         copy.wait()
 
@@ -252,7 +258,7 @@
     left_half = jnp.concatenate([stack[16 * b : 16 * b + 8] for b in range(4)], 0)
     message[...] = jnp.concatenate([left_half, right_half], 1).reshape(N_MEM, 1, WIDTH)
 
-    pl.semaphore_wait(barrier, N_MEM - 1 + N_TILE - 1)
+    pl.semaphore_wait(barrier, N_MEM - 1 + tile)
 
     def send_rows(c):
         def source(p):
@@ -282,6 +288,8 @@
     for c in range(CHUNKS):
         send_rows(c)
 
+    for q in tile_partners:
+        greet(q < tile, tile_ready, q)
     pltpu.make_async_copy(received, received, obs_recv).wait()
     arrived = received[...].reshape(N_MEM, WIDTH)
     arrived = jnp.concatenate([arrived, jnp.zeros((128 - N_MEM, WIDTH), F32)], 0).T
@@ -291,6 +299,11 @@
         )
     loads = jnp.sum(arrived[192 : 192 + N_TILE], 1, keepdims=True)
     load_send[...] = jnp.broadcast_to(loads, (N_TILE, 128)).reshape(N_TILE, 1, 128)
+
+    @pl.when(tile < N_TILE - 1)
+    def _():
+        pl.semaphore_wait(tile_ready, N_TILE - 1 - tile)
+
     for q in tile_partners:
         pltpu.make_async_remote_copy(
             src_ref=load_send.at[q],
@@ -386,6 +399,7 @@
             pltpu.VMEM((N_TILE, 1, 128), F32),
             pltpu.VMEM((CHUNKS, N_MEM, CHUNK, WIDTH), F32),
             pltpu.VMEM((CHUNKS, N_MEM, CHUNK, WIDTH), F32),
+            pltpu.SemaphoreType.REGULAR,
             dma((7,)),
             dma((CHUNKS,)),
             dma((CHUNKS,)),

time: 26.7 us -> 26.3 us (0.985)
  Pallas kernels: 25.9 us -> 25.5 us
    pallas_call x1, Pallas kernels: 25.1 us -> 24.7 us  [per_device(): pl.pallas_call(kernel, out_shape=(jax.ShapeDtypeStruct((COLS_T, WIDTH), F...]
where the time goes in v3:
time: 26.3 us; the launch traced here: 26.2 us
  Pallas kernels  25.5 us (97%)
  between operations  0.64 us (2%)
    pallas_call x1, Pallas kernels, per_device(): pl.pallas_call(kernel, out_shape=(jax.ShapeDtypeStruct((COLS_T, WIDTH), F...  24.7 us
    pallas_call x1, Pallas kernels, per_device(): pl.pallas_call(finish, out_shape=(jax.ShapeDtypeStruct((COLS_T, WIDTH), F...  0.81 us

profile of v3, /device:TPU:1, one launch (start us, length us, event | category | flops | bytes accessed | tf_op | source)
XLA Modules:
  0.0 26.2 jit_solution(13070191032587159357)
XLA Ops:
  0.6 24.7 %shard_map.95 = (f32[512,256]{1,0:T(8,128)S(1)}, f32[4,1,128]{2,1,0:T(1,128)S(1)}) custom-call(f32[512,256]{1,0:T(8,128)} %bg.1, f32[4,512]{1,0:T(4,128)} %bitcast.9, f32[4,512]{1,0:T(4,128)} %bitcast.10, f32[4,512]{1,0:T(4,128)} %bitcast.11, s32[4,512]{1,0:T(4,128)} %bitcast.12, s32[1,512]{1,0:T(1,128)} %bitcast.13, s32[1,512]{1,0:T(1,128)} %bitcast.14, ...), custom_call_target="tpu_custom_call" | custom-call | tf_op jit(solution)/shard_map/pallas_call | solution.py:379
  25.3 0.8 %shard_map.96 = (f32[512,256]{1,0:T(8,128)}, f32[1,128]{1,0:T(1,128)}) custom-call(f32[512,256]{1,0:T(8,128)S(1)} %get-tuple-element.6.rows, f32[4,1,128]{2,1,0:T(1,128)S(1)} %get-tuple-element.7.parts), custom_call_target="tpu_custom_call" | custom-call | tf_op jit(solution)/shard_map/pallas_call | solution.py:425

commit v4 on v3

--- a/solution.py
+++ b/solution.py
@@ -193,8 +193,8 @@
 def kernel(
     bg, value, height, obs_weight, index, counts, owner, table, out, load_recv,
     value_v, height_v, weight_v, index_v, counts_v, owner_v, table_v,
-    message, received, fields, shared, load_send, rows_in, rows_out,
-    tile_ready, small_sem, in_send, in_recv, out_send, out_recv, obs_send, obs_recv, load_sems,
+    message, received, fields, shared, load_send, rows_in, rows_out, rows_own,
+    tile_ready, small_sem, stage_sem, in_send, in_recv, out_send, out_recv, obs_send, obs_recv, load_sems,
 ):
     me = lax.axis_index("mem")
     tile = lax.axis_index("tile")
@@ -218,6 +218,8 @@
     ]
     for copy in small:
         copy.start()
+    stage = pltpu.make_async_copy(bg, rows_own, stage_sem)
+    stage.start()
     barrier = pltpu.get_barrier_semaphore()
     for p in partners:
         pl.semaphore_signal(barrier, inc=1, device_id=(p, tile), device_id_type=MESH)
@@ -258,22 +260,24 @@
     left_half = jnp.concatenate([stack[16 * b : 16 * b + 8] for b in range(4)], 0)
     message[...] = jnp.concatenate([left_half, right_half], 1).reshape(N_MEM, 1, WIDTH)
 
+    def source(c, p):
+        return rows_own.at[pl.ds(pl.multiple_of(p * OWN + c * CHUNK, CHUNK), CHUNK)]
+
+    stage.wait()
+    for c in range(CHUNKS):
+        pltpu.make_async_copy(source(c, me), rows_in.at[c, me], in_recv.at[c]).start()
     pl.semaphore_wait(barrier, N_MEM - 1 + tile)
 
     def send_rows(c):
-        def source(p):
-            return bg.at[pl.ds(pl.multiple_of(p * OWN + c * CHUNK, CHUNK), CHUNK)]
-
         for p in partners:
             pltpu.make_async_remote_copy(
-                src_ref=source(p),
+                src_ref=source(c, p),
                 dst_ref=rows_in.at[c, me],
                 send_sem=in_send.at[c],
                 recv_sem=in_recv.at[c],
                 device_id=(p, tile),
                 device_id_type=MESH,
             ).start()
-        pltpu.make_async_copy(source(me), rows_in.at[c, me], in_recv.at[c]).start()
 
     for p in partners:
         pltpu.make_async_remote_copy(
@@ -399,8 +403,10 @@
             pltpu.VMEM((N_TILE, 1, 128), F32),
             pltpu.VMEM((CHUNKS, N_MEM, CHUNK, WIDTH), F32),
             pltpu.VMEM((CHUNKS, N_MEM, CHUNK, WIDTH), F32),
+            pltpu.VMEM((COLS_T, WIDTH), F32),
             pltpu.SemaphoreType.REGULAR,
             dma((7,)),
+            dma,
             dma((CHUNKS,)),
             dma((CHUNKS,)),
             dma((CHUNKS,)),

time: 26.3 us -> 26.1 us (level)
  no operation moved by 1% of the time
where the time goes in v4:
time: 26.1 us; the launch traced here: 26 us
  Pallas kernels  25.3 us (97%)
  between operations  0.64 us (2%)
    pallas_call x1, Pallas kernels, per_device(): pl.pallas_call(kernel, out_shape=(jax.ShapeDtypeStruct((COLS_T, WIDTH), F...  24.5 us
    pallas_call x1, Pallas kernels, per_device(): pl.pallas_call(finish, out_shape=(jax.ShapeDtypeStruct((COLS_T, WIDTH), F...  0.81 us

profile of v4, /device:TPU:1, one launch (start us, length us, event | category | flops | bytes accessed | tf_op | source)
XLA Modules:
  0.0 26.0 jit_solution(3749287497141373028)
XLA Ops:
  0.6 24.5 %shard_map.95 = (f32[512,256]{1,0:T(8,128)S(1)}, f32[4,1,128]{2,1,0:T(1,128)S(1)}) custom-call(f32[512,256]{1,0:T(8,128)} %bg.1, f32[4,512]{1,0:T(4,128)} %bitcast.9, f32[4,512]{1,0:T(4,128)} %bitcast.10, f32[4,512]{1,0:T(4,128)} %bitcast.11, s32[4,512]{1,0:T(4,128)} %bitcast.12, s32[1,512]{1,0:T(1,128)} %bitcast.13, s32[1,512]{1,0:T(1,128)} %bitcast.14, ...), custom_call_target="tpu_custom_call" | custom-call | tf_op jit(solution)/shard_map/pallas_call | solution.py:383
  25.2 0.8 %shard_map.96 = (f32[512,256]{1,0:T(8,128)}, f32[1,128]{1,0:T(1,128)}) custom-call(f32[512,256]{1,0:T(8,128)S(1)} %get-tuple-element.6.rows, f32[4,1,128]{2,1,0:T(1,128)S(1)} %get-tuple-element.7.parts), custom_call_target="tpu_custom_call" | custom-call | tf_op jit(solution)/shard_map/pallas_call | solution.py:431

commit v5 on v4

--- a/solution.py
+++ b/solution.py
@@ -77,7 +77,7 @@
             shared[q, k] = jnp.where(left, both[0][k], both[1][k])
         return carry
 
-    lax.fori_loop(0, OWN // 2, pair, 0)
+    lax.fori_loop(0, OWN // 2, pair, 0, unroll=8)
 
 
 def analyse(blocks, shared):
@@ -301,24 +301,6 @@
         fields[f] = jnp.concatenate(
             [arrived[(4 * f + o) * OWN : (4 * f + o + 1) * OWN, :N_MEM] for o in range(OBS_L)], 1
         )
-    loads = jnp.sum(arrived[192 : 192 + N_TILE], 1, keepdims=True)
-    load_send[...] = jnp.broadcast_to(loads, (N_TILE, 128)).reshape(N_TILE, 1, 128)
-
-    @pl.when(tile < N_TILE - 1)
-    def _():
-        pl.semaphore_wait(tile_ready, N_TILE - 1 - tile)
-
-    for q in tile_partners:
-        pltpu.make_async_remote_copy(
-            src_ref=load_send.at[q],
-            dst_ref=load_recv.at[tile],
-            send_sem=load_sems.at[0],
-            recv_sem=load_sems.at[1],
-            device_id=(me, q),
-            device_id_type=MESH,
-        ).start()
-    pltpu.make_async_copy(load_send.at[tile], load_recv.at[tile], load_sems.at[1]).start()
-
     observe(fields, shared)
 
     def step(c, carry):
@@ -349,7 +331,28 @@
         pltpu.make_async_copy(rows_out.at[c, me], target, out_recv.at[c]).start()
         return carry
 
-    lax.fori_loop(0, CHUNKS, step, 0)
+    kept = jnp.sum(arrived[192 : 192 + N_TILE], 1, keepdims=True)
+    for c in range(CHUNKS):
+        step(c, 0)
+        if c == 0:
+            loads = kept
+            load_send[...] = jnp.broadcast_to(loads, (N_TILE, 128)).reshape(N_TILE, 1, 128)
+
+            @pl.when(tile < N_TILE - 1)
+            def _():
+                pl.semaphore_wait(tile_ready, N_TILE - 1 - tile)
+
+            for q in tile_partners:
+                pltpu.make_async_remote_copy(
+                    src_ref=load_send.at[q],
+                    dst_ref=load_recv.at[tile],
+                    send_sem=load_sems.at[0],
+                    recv_sem=load_sems.at[1],
+                    device_id=(me, q),
+                    device_id_type=MESH,
+                ).start()
+            pltpu.make_async_copy(load_send.at[tile], load_recv.at[tile], load_sems.at[1]).start()
+
 
     pltpu.make_async_copy(load_recv, load_recv, load_sems.at[1]).wait()
     sent = load_send.at[pl.ds(0, N_TILE - 1)]

time: 26.1 us -> 26.1 us (level)
  no operation moved by 1% of the time
where the time goes in v5:
time: 26.1 us; the launch traced here: 25.9 us
  Pallas kernels  25.3 us (97%)
  between operations  0.64 us (2%)
    pallas_call x1, Pallas kernels, per_device(): pl.pallas_call(kernel, out_shape=(jax.ShapeDtypeStruct((COLS_T, WIDTH), F...  24.5 us
    pallas_call x1, Pallas kernels, per_device(): pl.pallas_call(finish, out_shape=(jax.ShapeDtypeStruct((COLS_T, WIDTH), F...  0.81 us

profile of v5, /device:TPU:1, one launch (start us, length us, event | category | flops | bytes accessed | tf_op | source)
XLA Modules:
  0.0 25.9 jit_solution(2028842275896185915)
XLA Ops:
  0.6 24.5 %shard_map.95 = (f32[512,256]{1,0:T(8,128)S(1)}, f32[4,1,128]{2,1,0:T(1,128)S(1)}) custom-call(f32[512,256]{1,0:T(8,128)} %bg.1, f32[4,512]{1,0:T(4,128)} %bitcast.9, f32[4,512]{1,0:T(4,128)} %bitcast.10, f32[4,512]{1,0:T(4,128)} %bitcast.11, s32[4,512]{1,0:T(4,128)} %bitcast.12, s32[1,512]{1,0:T(1,128)} %bitcast.13, s32[1,512]{1,0:T(1,128)} %bitcast.14, ...), custom_call_target="tpu_custom_call" | custom-call | tf_op jit(solution)/shard_map/pallas_call | solution.py:386
  25.1 0.8 %shard_map.96 = (f32[512,256]{1,0:T(8,128)}, f32[1,128]{1,0:T(1,128)}) custom-call(f32[512,256]{1,0:T(8,128)S(1)} %get-tuple-element.6.rows, f32[4,1,128]{2,1,0:T(1,128)S(1)} %get-tuple-element.7.parts), custom_call_target="tpu_custom_call" | custom-call | tf_op jit(solution)/shard_map/pallas_call | solution.py:434

commit v6 on v5

--- a/solution.py
+++ b/solution.py
@@ -60,7 +60,7 @@
     return lane, iota((64, 128), 0), left, keep0, keep1
 
 
-def observe(fields, shared):
+def observe(fields, shared, first, count):
     left = lane_masks()[2]
     level = iota((64, 128), 0).astype(F32)
 
@@ -77,7 +77,8 @@
             shared[q, k] = jnp.where(left, both[0][k], both[1][k])
         return carry
 
-    lax.fori_loop(0, OWN // 2, pair, 0, unroll=8)
+    for q in range(first, first + count):
+        pair(q, 0)
 
 
 def analyse(blocks, shared):
@@ -296,12 +297,12 @@
         greet(q < tile, tile_ready, q)
     pltpu.make_async_copy(received, received, obs_recv).wait()
     arrived = received[...].reshape(N_MEM, WIDTH)
-    arrived = jnp.concatenate([arrived, jnp.zeros((128 - N_MEM, WIDTH), F32)], 0).T
+    arrived = arrived.T
     for f in range(3):
         fields[f] = jnp.concatenate(
             [arrived[(4 * f + o) * OWN : (4 * f + o + 1) * OWN, :N_MEM] for o in range(OBS_L)], 1
         )
-    observe(fields, shared)
+    observe(fields, shared, 0, CHUNK // 2)
 
     def step(c, carry):
         pltpu.make_async_copy(rows_in.at[c], rows_in.at[c], in_recv.at[c]).wait()
@@ -312,6 +313,8 @@
                 for q in range(CHUNK // 2)
             ],
         )
+        if c + 1 < CHUNKS:
+            observe(fields, shared, (c + 1) * (CHUNK // 2), CHUNK // 2)
         for i in range(CHUNK):
             rows_out[c, :, i, :] = results[i]
         target = out.at[pl.ds(pl.multiple_of(me * OWN + c * CHUNK, CHUNK), CHUNK)]

time: 26.1 us -> 26.1 us (level)
  no operation moved by 1% of the time
where the time goes in v6:
time: 26.1 us; the launch traced here: 26 us
  Pallas kernels  25.3 us (97%)
  between operations  0.64 us (2%)
    pallas_call x1, Pallas kernels, per_device(): pl.pallas_call(kernel, out_shape=(jax.ShapeDtypeStruct((COLS_T, WIDTH), F...  24.5 us
    pallas_call x1, Pallas kernels, per_device(): pl.pallas_call(finish, out_shape=(jax.ShapeDtypeStruct((COLS_T, WIDTH), F...  0.81 us

profile of v6, /device:TPU:1, one launch (start us, length us, event | category | flops | bytes accessed | tf_op | source)
XLA Modules:
  0.0 26.0 jit_solution(14458997241851480819)
XLA Ops:
  0.6 24.5 %shard_map.95 = (f32[512,256]{1,0:T(8,128)S(1)}, f32[4,1,128]{2,1,0:T(1,128)S(1)}) custom-call(f32[512,256]{1,0:T(8,128)} %bg.1, f32[4,512]{1,0:T(4,128)} %bitcast.9, f32[4,512]{1,0:T(4,128)} %bitcast.10, f32[4,512]{1,0:T(4,128)} %bitcast.11, s32[4,512]{1,0:T(4,128)} %bitcast.12, s32[1,512]{1,0:T(1,128)} %bitcast.13, s32[1,512]{1,0:T(1,128)} %bitcast.14, ...), custom_call_target="tpu_custom_call" | custom-call | tf_op jit(solution)/shard_map/pallas_call | solution.py:389
  25.2 0.8 %shard_map.96 = (f32[512,256]{1,0:T(8,128)}, f32[1,128]{1,0:T(1,128)}) custom-call(f32[512,256]{1,0:T(8,128)S(1)} %get-tuple-element.6.rows, f32[4,1,128]{2,1,0:T(1,128)S(1)} %get-tuple-element.7.parts), custom_call_target="tpu_custom_call" | custom-call | tf_op jit(solution)/shard_map/pallas_call | solution.py:437

commit v7 on v4

--- a/solution.py
+++ b/solution.py
@@ -296,7 +296,7 @@
         greet(q < tile, tile_ready, q)
     pltpu.make_async_copy(received, received, obs_recv).wait()
     arrived = received[...].reshape(N_MEM, WIDTH)
-    arrived = jnp.concatenate([arrived, jnp.zeros((128 - N_MEM, WIDTH), F32)], 0).T
+    arrived = arrived.T
     for f in range(3):
         fields[f] = jnp.concatenate(
             [arrived[(4 * f + o) * OWN : (4 * f + o + 1) * OWN, :N_MEM] for o in range(OBS_L)], 1

time: 26.1 us -> 26.1 us (level)
  no operation moved by 1% of the time
where the time goes in v7:
time: 26.1 us; the launch traced here: 26 us
  Pallas kernels  25.3 us (97%)
  between operations  0.64 us (2%)
    pallas_call x1, Pallas kernels, per_device(): pl.pallas_call(kernel, out_shape=(jax.ShapeDtypeStruct((COLS_T, WIDTH), F...  24.5 us
    pallas_call x1, Pallas kernels, per_device(): pl.pallas_call(finish, out_shape=(jax.ShapeDtypeStruct((COLS_T, WIDTH), F...  0.81 us

profile of v7, /device:TPU:1, one launch (start us, length us, event | category | flops | bytes accessed | tf_op | source)
XLA Modules:
  0.0 26.0 jit_solution(12138517509521210555)
XLA Ops:
  0.6 24.5 %shard_map.95 = (f32[512,256]{1,0:T(8,128)S(1)}, f32[4,1,128]{2,1,0:T(1,128)S(1)}) custom-call(f32[512,256]{1,0:T(8,128)} %bg.1, f32[4,512]{1,0:T(4,128)} %bitcast.9, f32[4,512]{1,0:T(4,128)} %bitcast.10, f32[4,512]{1,0:T(4,128)} %bitcast.11, s32[4,512]{1,0:T(4,128)} %bitcast.12, s32[1,512]{1,0:T(1,128)} %bitcast.13, s32[1,512]{1,0:T(1,128)} %bitcast.14, ...), custom_call_target="tpu_custom_call" | custom-call | tf_op jit(solution)/shard_map/pallas_call | solution.py:383
  25.2 0.8 %shard_map.96 = (f32[512,256]{1,0:T(8,128)}, f32[1,128]{1,0:T(1,128)}) custom-call(f32[512,256]{1,0:T(8,128)S(1)} %get-tuple-element.6.rows, f32[4,1,128]{2,1,0:T(1,128)S(1)} %get-tuple-element.7.parts), custom_call_target="tpu_custom_call" | custom-call | tf_op jit(solution)/shard_map/pallas_call | solution.py:431
